TPU v7x, 256 devices: a whole 4x4x8 slice. The times are simulated.
256 devices in a mesh: dp: 16 (over x, y_hi, core), ctx: 16 (over y_lo, z).
Axes of the slice: x: 4, y: 4 (y_hi: 2, y_lo: 2; y = y_hi * 2 + y_lo), z: 8, core: 2. Of those that a mesh axis runs over, the one named last changes fastest.
Arguments:
- queries: bfloat16 [16, 16384, 512], P('dp', 'ctx'), may hold values from -6 to 6
- keys: bfloat16 [16, 16384, 128], P('dp', 'ctx'), may hold values from -6 to 6
- values: bfloat16 [16, 16384, 128], P('dp', 'ctx'), may hold values from -6 to 6
- dest_replica: int32 [16, 256], P('dp', 'ctx'), may hold values from 0 to 15, as said below
- dest_slot: int32 [16, 256], P('dp', 'ctx'), may hold values from 0 to 255, as said below
- doc_lengths: int32 [16, 64], P('dp'), may hold values from 1 to 32, 256 in all within a row
- tile_mask: int32 [16, 256, 256], P('dp', 'ctx'), may hold values 0 or 1
Outputs:
- attended: bfloat16 [16, 16384, 512], P('dp', 'ctx')
Inputs may be any that keep to these rules, and one draw needn't show every extreme that they name: `dest_replica`: every block of a pack receives exactly one arriving block; a block keeps its shard along ctx (dest_slot // 16 equals the arriving block's own b // 16); the 16 blocks of one device go to every pack, 1 to each. `dest_slot`: see dest_replica. `doc_lengths`: they sum to 256 in every pack, and the largest is 32 in every pack.
All inputs are finite; a program needn't handle non-finite values. No bound on the sum of `tile_mask` on one device may be relied on, other than what follows from the above.
Results may differ from a plain program's by a relative error of at most 0.0033.
Values may be sent and summed in bfloat16 or wider, within the bound.
A program may use at most 64 MiB of HBM per device.

v0:
```python
import jax
import jax.numpy as jnp
from jax import lax
from jax.sharding import PartitionSpec as P

HEAD_WIDTH = 128
QUERY_HEADS = 4
KEY_VALUE_HEADS = 1
REACH = 2


def shifted(value, axis, steps):
    count = lax.axis_size(axis)
    leading, last = (max(0, -steps), min(count, count - steps))
    return lax.ppermute(value, axis, [(source, source + steps) for source in range(leading, last)])


def block_docs(ends, block_ids):
    return jnp.sum((ends[None, :] <= block_ids[:, None]).astype(jnp.int32), axis=1)


def shard_attend(rows_of_queries, rows_of_keys, rows_of_values, allowed):
    count_of_rows = rows_of_queries.shape[0]
    query_group_width = QUERY_HEADS // KEY_VALUE_HEADS
    heads_of_queries = rows_of_queries.reshape(
        count_of_rows, KEY_VALUE_HEADS, query_group_width, HEAD_WIDTH
    )
    heads_of_keys = rows_of_keys.reshape(rows_of_keys.shape[0], KEY_VALUE_HEADS, HEAD_WIDTH)
    heads_of_values = rows_of_values.reshape(rows_of_values.shape[0], KEY_VALUE_HEADS, HEAD_WIDTH)
    scores = jnp.einsum(
        "qhgd,khd->hgqk", heads_of_queries, heads_of_keys, preferred_element_type=jnp.float32
    ) * HEAD_WIDTH ** (-0.5)
    masked = jnp.where(allowed, scores, -jnp.inf)
    row_max = jnp.max(masked, axis=-1)
    present = jnp.any(allowed, axis=-1)
    safe_max = jnp.where(present, row_max, 0.0)
    weights = jnp.where(allowed, jnp.exp(scores - safe_max[..., None]), 0.0)
    row_sum = jnp.sum(weights, axis=-1)
    partial_value = jnp.einsum(
        "hgqk,khd->qhgd",
        weights.astype(jnp.bfloat16),
        heads_of_values,
        preferred_element_type=jnp.float32,
    )
    return (row_max, row_sum, partial_value)


def combine(portions):
    overall = portions[0][0]
    for portion in portions[1:]:
        overall = jnp.maximum(overall, portion[0])
    denominator = jnp.zeros_like(overall)
    numerator = jnp.zeros_like(portions[0][2])
    for portion in portions:
        factor = jnp.exp(portion[0] - overall)
        denominator = denominator + factor * portion[1]
        numerator = numerator + jnp.transpose(factor, (2, 0, 1))[..., None] * portion[2]
    result = numerator / jnp.transpose(denominator, (2, 0, 1))[..., None]
    return result.reshape(result.shape[0], -1).astype(jnp.bfloat16)


def per_device(queries, keys, values, dest_replica, dest_slot, doc_lengths, tile_mask):
    token_count = queries.shape[1]
    block_count = dest_replica.shape[1]
    block_len = token_count // block_count
    replica_count = lax.axis_size("dp")
    per_pack = block_count // replica_count
    column = lax.axis_index("ctx")
    targets = dest_replica[0]
    local_slot = dest_slot[0] - column * block_count
    block_index = jnp.arange(block_count, dtype=jnp.int32)
    same_target = targets[:, None] == targets[None, :]
    earlier = block_index[None, :] < block_index[:, None]
    ranking = jnp.sum((same_target & earlier).astype(jnp.int32), axis=1)
    select = targets[None, None, :] == jnp.arange(replica_count, dtype=jnp.int32)[:, None, None]
    select = select & (
        ranking[None, None, :] == jnp.arange(per_pack, dtype=jnp.int32)[None, :, None]
    )
    select_matrix = select.astype(jnp.bfloat16)
    slot_send = jnp.sum(select.astype(jnp.int32) * (local_slot + 1)[None, None, :], axis=2) - 1

    def pack_blocks(array):
        blocks = array[0].reshape(block_count, block_len, array.shape[2])
        return jnp.einsum(
            "kcj,jbf->kcbf", select_matrix, blocks, preferred_element_type=jnp.float32
        ).astype(jnp.bfloat16)

    def place_blocks(received, slots_in):
        placer = (slots_in[None, :, :] == block_index[:, None, None]).astype(jnp.bfloat16)
        placed = jnp.einsum(
            "jsc,scbf->jbf", placer, received, preferred_element_type=jnp.float32
        ).astype(jnp.bfloat16)
        return placed.reshape(token_count, received.shape[3])

    incoming_q, incoming_k, incoming_v, incoming_slots = (
        lax.all_to_all(pack_blocks(queries), "dp", split_axis=0, concat_axis=0, tiled=True),
        lax.all_to_all(pack_blocks(keys), "dp", split_axis=0, concat_axis=0, tiled=True),
        lax.all_to_all(pack_blocks(values), "dp", split_axis=0, concat_axis=0, tiled=True),
        lax.all_to_all(slot_send, "dp", split_axis=0, concat_axis=0, tiled=True),
    )
    routed_k = place_blocks(incoming_k, incoming_slots)
    routed_v = place_blocks(incoming_v, incoming_slots)
    routed_q = place_blocks(incoming_q, incoming_slots)
    ends = jnp.cumsum(doc_lengths[0])
    query_blocks = column * block_count + block_index
    query_docs = block_docs(ends, query_blocks)
    token_index = jnp.arange(token_count, dtype=jnp.int32)
    query_pos = column * token_count + token_index
    mask_rows = tile_mask[0]

    def allowed_for(offset):
        key_blocks = (column - offset) * block_count + block_index
        key_docs = block_docs(ends, key_blocks)
        start = jnp.maximum(column - offset, 0) * block_count
        mask_cols = lax.dynamic_slice_in_dim(mask_rows, start, block_count, 1)
        tile_ok = (query_docs[:, None] == key_docs[None, :]) & (
            key_blocks[None, :] <= query_blocks[:, None]
        )
        tile_ok = tile_ok & ((mask_cols == 1) | (key_blocks[None, :] == query_blocks[:, None]))
        tile_ok = tile_ok & (key_blocks[None, :] >= 0)
        expanded = jnp.repeat(jnp.repeat(tile_ok, block_len, axis=0), block_len, axis=1)
        key_pos = (column - offset) * token_count + token_index
        return expanded & (key_pos[None, :] <= query_pos[:, None])

    portions = [shard_attend(routed_q, routed_k, routed_v, allowed_for(0))]
    stacked_kv = jnp.stack((routed_k, routed_v))
    moving = stacked_kv
    for offset in range(1, REACH + 1):
        moving = shifted(moving, "ctx", 1)
        allowed = allowed_for(offset)
        portions.append(shard_attend(routed_q, moving[0], moving[1], allowed))
    return combine(portions)[None]


def solution(mesh):
    return jax.shard_map(
        per_device,
        mesh=mesh,
        in_specs=(
            P("dp", "ctx", None),
            P("dp", "ctx", None),
            P("dp", "ctx", None),
            P("dp", "ctx"),
            P("dp", "ctx"),
            P("dp", None),
            P("dp", "ctx", None),
        ),
        out_specs=P("dp", "ctx", None),
        check_vma=False,
    )
```

profile of v0, /device:TPU:8, one launch (start us, length us, event | category | flops | bytes accessed | tf_op | source)
XLA Modules:
  0.0 137.2 jit_solution(15221785307617733241)
XLA Ops:
  0.0 0.9 convert_reduce_fusion.2
  3.1 6.1 %all-to-all-start = ((s32[16,1,1]{2,1,0:T(1,128)}), s32[16,1,1]{2,1,0:T(1,128)S(1)}, u32[]{:S(2)}, u32[]{:S(2)}) async-start(s32[16,1,1]{2,1,0:T(1,128)} %copy.103), calls=%async_computation | async-start | bytes 16384 | tf_op jit(solution)/shard_map/all_to_all | solution.py:99
  10.2 1.2 fusion.35
  11.4 1.2 fusion.34
  13.7 3.1 %all-to-all-done = s32[16,1,1]{2,1,0:T(1,128)S(1)} async-done(((s32[16,1,1]{2,1,0:T(1,128)}), s32[16,1,1]{2,1,0:T(1,128)S(1)}, u32[]{:S(2)}, u32[]{:S(2)}) %all-to-all-start) | async-done | bytes 96 | tf_op jit(solution)/shard_map/all_to_all | solution.py:99
  16.8 4.1 %all-to-all-start.3 = ((bf16[16,1,64,128]{3,2,1,0:T(8,128)(2,1)}), bf16[16,1,64,128]{3,2,1,0:T(8,128)(2,1)S(1)}, u32[]{:S(2)}, u32[]{:S(2)}) async-start(bf16[16,1,64,128]{3,2,1,0:T(8,128)(2,1)} %copy.116), calls=%async_computation.3 | async-start | bytes 524288 | tf_op jit(solution)/shard_map/all_to_all | solution.py:98
  21.7 0.9 fusion.63
  22.6 7.5 %all-to-all-done.3 = bf16[16,1,64,128]{3,2,1,0:T(8,128)(2,1)S(1)} async-done(((bf16[16,1,64,128]{3,2,1,0:T(8,128)(2,1)}), bf16[16,1,64,128]{3,2,1,0:T(8,128)(2,1)S(1)}, u32[]{:S(2)}, u32[]{:S(2)}) %all-to-all-start.3) | async-done | bytes 262176 | tf_op jit(solution)/shard_map/all_to_all | solution.py:98
  30.1 4.2 %all-to-all-start.1 = ((bf16[16,1,64,128]{3,2,1,0:T(8,128)(2,1)}), bf16[16,1,64,128]{3,2,1,0:T(8,128)(2,1)}, u32[]{:S(2)}, u32[]{:S(2)}) async-start(bf16[16,1,64,128]{3,2,1,0:T(8,128)(2,1)} %copy.105), calls=%async_computation.1 | async-start | bytes 524288 | tf_op jit(solution)/shard_map/all_to_all | solution.py:97
  34.3 1.4 %fusion.33 = bf16[16,1,64,512]{3,0,2,1:T(8,128)(2,1)S(1)} fusion(bf16[16,64,512]{2,1,0:T(8,128)(2,1)S(1)} %bitcast.283, s32[16]{0:T(128)} %bitcast.295, pred[16]{0:T(512)(128)(4,1)S(1)} %get-tuple-element.29), kind=kOutput, calls=%fused_computation.45 | convolution fusion | flops 17302016 | bytes 2097232 | tf_op jit(solution)/shard_map/kcj,jbf->kcbf/dot_general | solution.py:84
  36.6 1.5 %copy.109 = bf16[16,1,64,512]{3,2,1,0:T(8,128)(2,1)} copy(bf16[16,1,64,512]{3,0,2,1:T(8,128)(2,1)S(1)} %fusion.33) | data formatting | bytes 2097152 | tf_op jit(solution)/shard_map/convert_element_type | solution.py:86
  38.2 2.5 %bitcast_and_fusion = (pred[1024,1024]{0,1:T(8,128)(4,1)S(1)}, pred[1024,1024]{0,1:T(8,128)(4,1)S(1)}, pred[1024,1024]{0,1:T(8,128)(4,1)S(1)}) fusion(s32[1024]{0:T(1024)S(1)} %iota_add_fusion.2, s32[1024]{0:T(1024)S(1)} %get-tuple-element.33, pred[1024,16]{0,1:T(8,128)(4,1)S(1)} %reshape.735, pred[1024,16]{0,1:T(8,128)(4,1)S(1)} %reshape.725, ...), kind=kLoop, calls=%fused_computation.30 | loop fusion | flops 6291456 | bytes 3207168 | tf_op jit(solution)/shard_map/and | solution.py:123
  41.1 2.4 %all-to-all-done.1 = bf16[16,1,64,128]{3,2,1,0:T(8,128)(2,1)} async-done(((bf16[16,1,64,128]{3,2,1,0:T(8,128)(2,1)}), bf16[16,1,64,128]{3,2,1,0:T(8,128)(2,1)}, u32[]{:S(2)}, u32[]{:S(2)}) %all-to-all-start.1) | async-done | bytes 262176 | tf_op jit(solution)/shard_map/all_to_all | solution.py:97
  43.5 4.7 %all-to-all-start.2 = ((bf16[16,1,64,512]{3,2,1,0:T(8,128)(2,1)}), bf16[16,1,64,512]{3,2,1,0:T(8,128)(2,1)}, u32[]{:S(2)}, u32[]{:S(2)}) async-start(bf16[16,1,64,512]{3,2,1,0:T(8,128)(2,1)} %copy.109), calls=%async_computation.2 | async-start | bytes 2097152 | tf_op jit(solution)/shard_map/all_to_all | solution.py:96
  48.6 1.2 convolution_convert_fusion.4
  50.7 3.8 %collective-permute-start = (bf16[2,1024,128]{2,1,0:T(8,128)(2,1)S(1)}, bf16[2,1024,128]{2,1,0:T(8,128)(2,1)}, u32[]{:S(2)}, u32[]{:S(2)}) collective-permute-start(bf16[2,1024,128]{2,1,0:T(8,128)(2,1)S(1)} %pad_maximum_fusion), channel_id=1, source_target_pairs={{0,1},{1,2},{2,3},{3,4},{4,5},{5,6},{6,7},{7,8},{8,9},{9,10},{10,1... | collective-permute-start | bytes 1572872 | tf_op jit(solution)/shard_map/ppermute | solution.py:15
  54.5 2.4 %and_reduce_fusion = (pred[1024]{0:T(1024)(128)(4,1)S(1)}, pred[1024]{0:T(1024)(128)(4,1)S(1)}, pred[1024]{0:T(1024)(128)(4,1)S(1)}) fusion(s32[16,64]{1,0:T(8,128)S(1)} %get-tuple-element.35, s32[1024]{0:T(1024)S(1)} %iota_add_fusion.2, pred[1024,16]{0,1:T(8,128)(4,1)S(1)} %reshape.735, s32[16,64]{1,0:T(8,128)S(1)} %get-tuple-element.36, ...), kind=kLoop, calls=%fused_computation.33 | loop fusion | flops 9434112 | bytes 68608 | tf_op jit(solution)/shard_map/reduce_or | solution.py:35
  57.0 18.7 %collective-permute-done = bf16[2,1024,128]{2,1,0:T(8,128)(2,1)} collective-permute-done((bf16[2,1024,128]{2,1,0:T(8,128)(2,1)S(1)}, bf16[2,1024,128]{2,1,0:T(8,128)(2,1)}, u32[]{:S(2)}, u32[]{:S(2)}) %collective-permute-start) | collective-permute-done | bytes 524320 | tf_op jit(solution)/shard_map/ppermute | solution.py:15
  75.7 2.1 %collective-permute-start.1 = (bf16[2,1024,128]{2,1,0:T(8,128)(2,1)}, bf16[2,1024,128]{2,1,0:T(8,128)(2,1)}, u32[]{:S(2)}, u32[]{:S(2)}) collective-permute-start(bf16[2,1024,128]{2,1,0:T(8,128)(2,1)} %collective-permute-done), channel_id=1, source_target_pairs={{0,1},{1,2},{2,3},{3,4},{4,5},{5,6},{6,7},{7,8},{8,9},{9,10},{10,1... | collective-permute-start | bytes 1572872 | tf_op jit(solution)/shard_map/ppermute | solution.py:15
  77.8 1.9 %convolution_convert_fusion = bf16[16,64,512]{2,0,1:T(8,128)(2,1)S(1)} fusion(bf16[16,1,64,512]{3,2,1,0:T(8,128)(2,1)} %all-to-all-done.2, s32[16]{0:T(128)S(1)} %reduce.11), kind=kOutput, calls=%fused_computation.43 | convolution fusion | flops 17301760 | bytes 2097216 | tf_op jit(solution)/shard_map/jsc,scbf->jbf/dot_general | solution.py:90
  79.8 1.5 %copy.111 = bf16[16,64,512]{2,1,0:T(8,128)(2,1)} copy(bf16[16,64,512]{2,0,1:T(8,128)(2,1)S(1)} %convolution_convert_fusion) | data formatting | bytes 2097152 | tf_op jit(solution)/shard_map/convert_element_type | solution.py:92
  81.3 2.2 %reshape.730 = bf16[1024,4,128]{2,1,0:T(4,128)(2,1)} reshape(bf16[16,64,512]{2,1,0:T(8,128)(2,1)} %copy.111) | data formatting | bytes 2097152 | tf_op jit(solution)/shard_map/reshape.27
  83.5 4.4 %fusion.6 = (f32[4,1024]{1,0:T(4,128)S(1)}, f32[1024,1024,4]{1,0,2:T(8,128)S(1)}) fusion(pred[1024,1024]{0,1:T(8,128)(4,1)S(1)} %get-tuple-element.19, bf16[1024,128,1]{1,0,2:T(8,128)(2,1)} %bitcast.288, bf16[1024,4,128]{2,1,0:T(4,128)(2,1)} %reshape.730), kind=kOutput, calls=%fused_computation.12 | convolution fusion | flops 1086320640 | bytes 19152896 | tf_op jit(solution)/shard_map/qhgd,khd->hgqk/dot_general | solution.py:30
  87.9 3.7 %fusion.9 = f32[4,1024]{1,0:T(4,128)S(1)} fusion(f32[1024,1024,4]{1,0,2:T(8,128)S(1)} %get-tuple-element.24, f32[4,1024]{1,0:T(4,128)S(1)} %broadcast_select_fusion.2, pred[1024,1024]{0,1:T(8,128)(4,1)S(1)} %get-tuple-element.19), kind=kLoop, calls=%fused_computation.15 | loop fusion | flops 16773120 | bytes 17858560 | tf_op jit(solution)/shard_map/reduce_sum | solution.py:38
  91.6 8.4 %fusion.3 = (f32[4,1024]{1,0:T(4,128)S(1)}, f32[1024,1024,4]{1,0,2:T(8,128)}) fusion(pred[1024,1024]{0,1:T(8,128)(4,1)S(1)} %get-tuple-element.20, bf16[1024,4,128]{2,1,0:T(4,128)(2,1)S(1)} %copy-done.2, bf16[2,1024,128]{2,1,0:T(8,128)(2,1)} %collective-permute-done), kind=kOutput, calls=%fused_computation.7 | convolution fusion | flops 1086320640 | bytes 19152896 | tf_op jit(solution)/shard_map/qhgd,khd->hgqk/dot_general | solution.py:30
  100.0 7.9 %fusion.11 = f32[4,1024]{1,0:T(4,128)S(1)} fusion(f32[1024,1024,4]{1,0,2:T(8,128)} %get-tuple-element.22, f32[4,1024]{1,0:T(4,128)S(1)} %broadcast_select_fusion.1, pred[1024,1024]{0,1:T(8,128)(4,1)S(1)} %get-tuple-element.20), kind=kLoop, calls=%fused_computation.17 | loop fusion | flops 16773120 | bytes 17858560 | tf_op jit(solution)/shard_map/reduce_sum | solution.py:38
  107.9 11.0 %fusion.20 = f32[128,4,1024]{2,0,1:T(8,128)} fusion(f32[1024,1024,4]{1,0,2:T(8,128)} %get-tuple-element.22, f32[4,1024]{1,0:T(4,128)S(1)} %broadcast_select_fusion.1, pred[1024,1024]{0,1:T(8,128)(4,1)S(1)} %get-tuple-element.20, bf16[2,1024,128]{2,1,0:T(8,128)(2,1)} %collective-permute-done), kind=kOutput, calls=%fused_computation.25 | convolution fusion | flops 1090519040 | bytes 20201472 | tf_op jit(solution)/shard_map/hgqk,khd->qhgd/dot_general | solution.py:39
  118.9 3.9 %fusion.18 = f32[128,4,1024]{2,0,1:T(8,128)S(1)} fusion(bf16[1024,128,1]{1,0,2:T(8,128)(2,1)S(1)} %bitcast.286, f32[1024,1024,4]{1,0,2:T(8,128)S(1)} %get-tuple-element.24, f32[4,1024]{1,0:T(4,128)S(1)} %broadcast_select_fusion.2, pred[1024,1024]{0,1:T(8,128)(4,1)S(1)} %get-tuple-element.19), kind=kOutput, calls=%fused_computation.24 | convolution fusion | flops 1090519040 | bytes 20201472 | tf_op jit(solution)/shard_map/hgqk,khd->qhgd/dot_general | solution.py:39
  122.9 4.0 %fusion = (f32[4,1024]{1,0:T(4,128)S(1)}, f32[1024,1024,4]{1,0,2:T(8,128)S(1)}) fusion(pred[1024,1024]{0,1:T(8,128)(4,1)S(1)} %get-tuple-element.18, bf16[1024,4,128]{2,1,0:T(4,128)(2,1)S(1)} %copy-done.2, bf16[2,1024,128]{2,1,0:T(8,128)(2,1)} %collective-permute-done.1), kind=kOutput, calls=%fused_computation.2 | convolution fusion | flops 1086320640 | bytes 19152896 | tf_op jit(solution)/shard_map/qhgd,khd->hgqk/dot_general | solution.py:30
  126.9 3.7 %fusion.13 = f32[4,1024]{1,0:T(4,128)S(1)} fusion(f32[1024,1024,4]{1,0,2:T(8,128)S(1)} %get-tuple-element.26, f32[4,1024]{1,0:T(4,128)S(1)} %broadcast_select_fusion, pred[1024,1024]{0,1:T(8,128)(4,1)S(1)} %get-tuple-element.18), kind=kLoop, calls=%fused_computation.19 | loop fusion | flops 16773120 | bytes 17858560 | tf_op jit(solution)/shard_map/reduce_sum | solution.py:38
  130.6 5.2 %fusion.29 = bf16[1024,1,4,128]{0,3,2,1:T(8,128)(2,1)S(1)} fusion(f32[128,4,1024]{2,0,1:T(8,128)S(1)} %copy-done.4, f32[128,4,1024]{2,0,1:T(8,128)S(1)} %fusion.18, f32[1024,1024,4]{1,0,2:T(8,128)S(1)} %get-tuple-element.26, f32[4,1024]{1,0:T(4,128)S(1)} %broadcast_select_fusion, pred[1024,1024]{0,1:T(8,128)(4,1)S(1)} %get-tuple-element.18, ...), kind=kOutput, calls=%fused_computation.39 | convolution fusion | flops 1094189056 | bytes 23412736 | tf_op jit(solution)/shard_map/hgqk,khd->qhgd/dot_general | solution.py:39
  135.8 1.3 copy.129
  (48 shorter events, 7.4 us)
Async XLA Ops:
  0.0 34.3 %copy-start = (bf16[1,1024,512]{2,1,0:T(8,128)(2,1)S(1)}, bf16[1,1024,512]{2,1,0:T(8,128)(2,1)}, u32[]{:S(2)}) copy-start(bf16[1,1024,512]{2,1,0:T(8,128)(2,1)} %param.7) | copy-start | bytes 3145732
  3.1 13.7 %all-to-all-start = ((s32[16,1,1]{2,1,0:T(1,128)}), s32[16,1,1]{2,1,0:T(1,128)S(1)}, u32[]{:S(2)}, u32[]{:S(2)}) async-start(s32[16,1,1]{2,1,0:T(1,128)} %copy.103), calls=%async_computation | async-start | bytes 16384 | tf_op jit(solution)/shard_map/all_to_all | solution.py:99
  16.8 13.3 %all-to-all-start.3 = ((bf16[16,1,64,128]{3,2,1,0:T(8,128)(2,1)}), bf16[16,1,64,128]{3,2,1,0:T(8,128)(2,1)S(1)}, u32[]{:S(2)}, u32[]{:S(2)}) async-start(bf16[16,1,64,128]{3,2,1,0:T(8,128)(2,1)} %copy.116), calls=%async_computation.3 | async-start | bytes 524288 | tf_op jit(solution)/shard_map/all_to_all | solution.py:98
  30.1 13.4 %all-to-all-start.1 = ((bf16[16,1,64,128]{3,2,1,0:T(8,128)(2,1)}), bf16[16,1,64,128]{3,2,1,0:T(8,128)(2,1)}, u32[]{:S(2)}, u32[]{:S(2)}) async-start(bf16[16,1,64,128]{3,2,1,0:T(8,128)(2,1)} %copy.105), calls=%async_computation.1 | async-start | bytes 524288 | tf_op jit(solution)/shard_map/all_to_all | solution.py:97
  43.5 34.3 %all-to-all-start.2 = ((bf16[16,1,64,512]{3,2,1,0:T(8,128)(2,1)}), bf16[16,1,64,512]{3,2,1,0:T(8,128)(2,1)}, u32[]{:S(2)}, u32[]{:S(2)}) async-start(bf16[16,1,64,512]{3,2,1,0:T(8,128)(2,1)} %copy.109), calls=%async_computation.2 | async-start | bytes 2097152 | tf_op jit(solution)/shard_map/all_to_all | solution.py:96
  49.9 0.7 copy-start.3
  50.7 25.0 %collective-permute-start = (bf16[2,1024,128]{2,1,0:T(8,128)(2,1)S(1)}, bf16[2,1024,128]{2,1,0:T(8,128)(2,1)}, u32[]{:S(2)}, u32[]{:S(2)}) collective-permute-start(bf16[2,1024,128]{2,1,0:T(8,128)(2,1)S(1)} %pad_maximum_fusion), channel_id=1, source_target_pairs={{0,1},{1,2},{2,3},{3,4},{4,5},{5,6},{6,7},{7,8},{8,9},{9,10},{10,1... | collective-permute-start | bytes 1572872 | tf_op jit(solution)/shard_map/ppermute | solution.py:15
  75.7 47.2 %collective-permute-start.1 = (bf16[2,1024,128]{2,1,0:T(8,128)(2,1)}, bf16[2,1024,128]{2,1,0:T(8,128)(2,1)}, u32[]{:S(2)}, u32[]{:S(2)}) collective-permute-start(bf16[2,1024,128]{2,1,0:T(8,128)(2,1)} %collective-permute-done), channel_id=1, source_target_pairs={{0,1},{1,2},{2,3},{3,4},{4,5},{5,6},{6,7},{7,8},{8,9},{9,10},{10,1... | collective-permute-start | bytes 1572872 | tf_op jit(solution)/shard_map/ppermute | solution.py:15
  83.5 8.1 %copy-start.2 = (bf16[1024,4,128]{2,1,0:T(4,128)(2,1)S(1)}, bf16[1024,4,128]{2,1,0:T(4,128)(2,1)}, u32[]{:S(2)}) copy-start(bf16[1024,4,128]{2,1,0:T(4,128)(2,1)} %reshape.730) | copy-start | bytes 3145732
  126.9 3.7 %copy-start.4 = (f32[128,4,1024]{2,0,1:T(8,128)S(1)}, f32[128,4,1024]{2,0,1:T(8,128)}, u32[]{:S(2)}) copy-start(f32[128,4,1024]{2,0,1:T(8,128)} %fusion.20) | copy-start | bytes 6291460
  130.6 6.6 %copy-start.1 = (bf16[1,1024,512]{2,1,0:T(8,128)(2,1)S(1)}, bf16[1,1024,512]{2,1,0:T(8,128)(2,1)}, u32[]{:S(2)}) copy-start(bf16[1,1024,512]{2,1,0:T(8,128)(2,1)} %param.7) | copy-start | bytes 3145732
where the time goes:
time: 138 us; the launch traced here: 137 us
  matrix products  44.2 us (32%)
  waiting for transfers between devices  31.8 us (23%)
  starting transfers between devices  25.1 us (18%)
  other arithmetic  24.4 us (18%)
  local copies, waits for them, and re-layouts  11.3 us (8%)
    dot_general x3, matrix products, shard_attend(): jnp.einsum('hgqk,khd->qhgd', weights.astype(jnp.bfloat16), heads_of_value...  20.1 us
    ppermute x2, waiting for transfers between devices, shifted(): lax.ppermute(value, axis, [(source, source + steps) for source in range(l...  18.7 us
    dot_general x3, matrix products, shard_attend(): jnp.einsum('qhgd,khd->hgqk', heads_of_queries, heads_of_keys, preferred_e...  16.8 us
    reduce_sum x3, other arithmetic, shard_attend(): row_sum = jnp.sum(weights, axis=-1)  15.3 us
    all_to_all x1, waiting for transfers between devices, per_device(): lax.all_to_all(pack_blocks(values), 'dp', split_axis=0, concat_axis=0, ti...  7.55 us
    all_to_all x1, starting transfers between devices, per_device(): lax.all_to_all(slot_send, 'dp', split_axis=0, concat_axis=0, tiled=True)  6.14 us
    ppermute x2, starting transfers between devices, shifted(): lax.ppermute(value, axis, [(source, source + steps) for source in range(l...  5.93 us
    all_to_all x1, starting transfers between devices, per_device(): lax.all_to_all(pack_blocks(queries), 'dp', split_axis=0, concat_axis=0, t...  4.72 us
  transfers between devices with their start and end apart: 6, of which 4 were waited for; matrix products, arithmetic and copies ran while one was open for 45% of the time, Pallas kernels for 0%

commit v1 on v0

v1 whole, which is shorter than its diff:
```python
import functools

import jax
import jax.numpy as jnp
from jax import lax
from jax.experimental import pallas as pl
from jax.experimental.pallas import tpu as pltpu
from jax.sharding import PartitionSpec as P

MESH = pl.DeviceIdType.MESH
HEADS = 4
WIDTH = 128
BLK = 64
NB = 16
TOK = NB * BLK
ROWS = HEADS * BLK
KEYS = 256
SCALE = WIDTH ** (-0.5) * 1.4426950408889634
LOW = -32768.0
CHUNKS = 4
PER = NB // CHUNKS


def tile_bias(col, docs_ref, mask_ref):
    count = docs_ref.shape[1]
    blocks = mask_ref.shape[1]
    lengths = docs_ref[...].astype(jnp.float32)
    upto = lax.broadcasted_iota(jnp.int32, (count, count), 1) <= lax.broadcasted_iota(jnp.int32, (count, count), 0)
    ends = jnp.sum(jnp.where(upto, jnp.broadcast_to(lengths, (count, count)), 0.0), axis=1, keepdims=True)
    block = lax.broadcasted_iota(jnp.int32, (count, blocks), 1).astype(jnp.float32)
    key_doc = jnp.sum(jnp.where(ends <= block, 1.0, 0.0), axis=0, keepdims=True)
    key_doc = jnp.broadcast_to(key_doc, (NB, blocks))
    key_block = lax.broadcasted_iota(jnp.int32, (NB, blocks), 1)
    query_block = lax.broadcasted_iota(jnp.int32, (NB, blocks), 0) + col * NB
    own = key_block == query_block
    query_doc = jnp.sum(jnp.where(own, key_doc, 0.0), axis=1, keepdims=True)
    ok = (key_doc == query_doc) & (key_block <= query_block) & ((mask_ref[...] == 1) | own)
    ok = jnp.where(ok, 1.0, 0.0).astype(jnp.bfloat16)
    window = lax.broadcasted_iota(jnp.int32, (blocks, 128), 1) + (col - 2) * NB
    pick = jnp.where(lax.broadcasted_iota(jnp.int32, (blocks, 128), 0) == window, 1.0, 0.0).astype(jnp.bfloat16)
    ok = jnp.dot(ok, pick, preferred_element_type=jnp.float32)
    return ((1.0 - ok) * LOW).astype(jnp.bfloat16)


def kernel(
    n, columns, q_ref, k_ref, v_ref, rep_ref, rep_vec, slot_vec, docs_ref, mask_ref, out_ref,
    kv_send, kv_recv, q_send, q_recv, code_send, code_recv, halo, q_aug, k_aug, v_aug, bias, acc, top, src,
    kv_sent, kv_got, q_sent, q_got, code_sent, code_got, halo_sent, halo_got,
):
    me = lax.axis_index("dp")
    col = lax.axis_index("ctx")
    right = lax.rem(col + 1, columns)
    left = lax.rem(col + columns - 1, columns)

    barrier = pltpu.get_barrier_semaphore()

    def greet(d, carry):
        pl.semaphore_signal(barrier, inc=1, device_id={"dp": lax.rem(me + d, n)}, device_id_type=MESH)
        return carry

    lax.fori_loop(1, n, greet, 0)
    pl.semaphore_signal(barrier, inc=1, device_id={"ctx": right}, device_id_type=MESH)
    pl.semaphore_signal(barrier, inc=1, device_id={"ctx": left}, device_id_type=MESH)

    code_send[...] = jnp.full((1, 128), -1, jnp.int32)
    code_send[:, :NB] = rep_vec[...] * NB + slot_vec[...] - col * NB

    def block_for(peer):
        where = jnp.int32(0)
        for j in range(NB):
            where = jnp.where(rep_ref[0, j] == peer, j, where)
        return where

    def pack_kv(peer, carry):
        j = block_for(peer)
        kv_send[peer, 0] = k_ref[j]
        kv_send[peer, 1] = v_ref[j]
        return carry

    lax.fori_loop(0, n, pack_kv, 0)

    def kv_copy(peer, slot):
        return pltpu.make_async_remote_copy(
            src_ref=kv_send.at[peer], dst_ref=kv_recv.at[slot], send_sem=kv_sent.at[peer],
            recv_sem=kv_got.at[slot], device_id={"dp": peer}, device_id_type=MESH)

    def q_copy(peer, slot):
        return pltpu.make_async_remote_copy(
            src_ref=q_send.at[peer], dst_ref=q_recv.at[slot], send_sem=q_sent.at[peer],
            recv_sem=q_got.at[slot], device_id={"dp": peer}, device_id_type=MESH)

    def code_copy(peer, slot):
        return pltpu.make_async_remote_copy(
            src_ref=code_send, dst_ref=code_recv.at[slot], send_sem=code_sent.at[peer],
            recv_sem=code_got.at[slot], device_id={"dp": peer}, device_id_type=MESH)

    pl.semaphore_wait(barrier, n + 1)

    def send_kv(d, carry):
        peer = lax.rem(me + d, n)
        code_copy(peer, me).start()
        kv_copy(peer, me).start()
        return carry

    lax.fori_loop(1, n, send_kv, 0)

    def send_q(d, carry):
        peer = lax.rem(me + d, n)
        q_send[peer] = q_ref[block_for(peer)]
        q_copy(peer, me).start()
        return carry

    lax.fori_loop(1, n, send_q, 0)
    mine = block_for(me)
    q_recv[me] = q_ref[mine]
    kv_recv[me, 0] = k_ref[mine]
    kv_recv[me, 1] = v_ref[mine]
    code_recv[me] = code_send[...]

    rows = tile_bias(col, docs_ref, mask_ref).astype(jnp.float32)
    for i in range(NB):
        bias[i] = jnp.broadcast_to(rows[i:i + 1], (16, 128)).astype(jnp.bfloat16)
    key_at = lax.broadcasted_iota(jnp.int32, (TOK, 128), 0) // BLK
    lane = lax.broadcasted_iota(jnp.int32, (TOK, 128), 1)
    for p in range(3):
        k_aug[p, :, WIDTH:] = jnp.where(lane == key_at + (2 - p) * NB, 1.0, 0.0).astype(jnp.bfloat16)
        v_aug[p, :, WIDTH:] = jnp.ones((TOK, 128), jnp.bfloat16)

    def got_kv(d, carry):
        peer = lax.rem(me + n - d, n)
        code_copy(peer, peer).wait_recv()
        kv_copy(peer, peer).wait_recv()
        return carry

    lax.fori_loop(1, n, got_kv, 0)
    codes = code_recv[...].reshape(n, 128)
    sender = lax.broadcasted_iota(jnp.int32, (n, 128), 0)
    for i in range(NB):
        src[i] = jnp.max(jnp.where(codes == me * NB + i, sender, 0))

    def place_kv(i, carry):
        s = src[i]
        rows = pl.ds(pl.multiple_of(i * BLK, BLK), BLK)
        key, value = kv_recv[s, 0], kv_recv[s, 1]
        halo[0, i, 0] = key
        halo[0, i, 1] = value
        k_aug[0, rows, :WIDTH] = key
        v_aug[0, rows, :WIDTH] = value
        return carry

    lax.fori_loop(0, NB, place_kv, 0)

    def halo_copy(hop, chunk):
        part = pl.ds(chunk * PER, PER)
        return pltpu.make_async_remote_copy(
            src_ref=halo.at[hop, part], dst_ref=halo.at[hop + 1, part], send_sem=halo_sent.at[hop, chunk],
            recv_sem=halo_got.at[hop, chunk], device_id={"ctx": right}, device_id_type=MESH)

    for chunk in range(CHUNKS):
        halo_copy(0, chunk).start()

    def got_q(d, carry):
        peer = lax.rem(me + n - d, n)
        q_copy(peer, peer).wait_recv()
        return carry

    lax.fori_loop(1, n, got_q, 0)

    def attend(i, p, lo, hi, diag=None):
        if p == 0:
            block = q_recv[src[i]]
            heads = jnp.concatenate([block[:, h * WIDTH:(h + 1) * WIDTH] for h in range(HEADS)], axis=0)
            query = jnp.concatenate([heads, jnp.concatenate([bias[i]] * (ROWS // 16), axis=0)], axis=1)
            q_aug[i] = query
        else:
            query = q_aug[i]
        score = lax.dot_general(
            query, k_aug[p, lo:hi, :], (((1,), (1,)), ((), ())), preferred_element_type=jnp.float32)
        if diag is not None:
            at = lax.rem(lax.broadcasted_iota(jnp.int32, (ROWS, KEYS), 0), BLK) + diag * BLK
            last = jnp.where(lax.broadcasted_iota(jnp.int32, (ROWS, KEYS), 1) <= at, score[:, -KEYS:], LOW)
            score = last if hi - lo == KEYS else jnp.concatenate([score[:, :-KEYS], last], axis=1)
        high = jnp.broadcast_to(jnp.max(score, axis=1, keepdims=True), (ROWS, 128))
        if p > 0:
            before = top[i]
            high = jnp.maximum(high, before)
        weight = jnp.exp2((score - jnp.concatenate([high] * ((hi - lo) // 128), axis=1)) * SCALE)
        part = jnp.dot(weight.astype(jnp.bfloat16), v_aug[p, lo:hi, :], preferred_element_type=jnp.float32)
        if p > 0:
            factor = jnp.exp2((before - high) * SCALE)
            part = part + acc[i] * jnp.concatenate([factor, factor], axis=1)
        if p < 2:
            acc[i] = part
            top[i] = high
        else:
            result = (part[:, :WIDTH] / part[:, WIDTH:]).astype(jnp.bfloat16)
            for h in range(HEADS):
                out_ref[i, :, h * WIDTH:(h + 1) * WIDTH] = result[h * BLK:(h + 1) * BLK]

    def sweep(p, first, count, lo, hi, diag=False):
        def step(j, carry):
            attend(first + j, p, lo, hi, j if diag else None)
            return carry

        lax.fori_loop(0, count, step, 0)

    def take_halo(hop):
        def place(i, carry):
            rows = pl.ds(pl.multiple_of(i * BLK, BLK), BLK)
            k_aug[hop, rows, :WIDTH] = halo[hop, i, 0]
            v_aug[hop, rows, :WIDTH] = halo[hop, i, 1]
            return carry

        lax.fori_loop(0, NB, place, 0)

    for g in range(4):
        sweep(0, g * 4, 4, 0, (g + 1) * KEYS, True)
        halo_copy(0, g).wait_recv()
        halo_copy(1, g).start()
    take_halo(1)
    sweep(1, 0, NB, 0, TOK)
    for chunk in range(CHUNKS):
        halo_copy(1, chunk).wait_recv()
    take_halo(2)
    sweep(2, 0, 3, 0, TOK)
    sweep(2, 3, 4, KEYS, TOK)
    sweep(2, 7, 4, 2 * KEYS, TOK)
    sweep(2, 11, 5, 3 * KEYS, TOK)

    for chunk in range(CHUNKS):
        halo_copy(0, chunk).wait_send()
        halo_copy(1, chunk).wait_send()

    def sent(d, carry):
        peer = lax.rem(me + d, n)
        code_copy(peer, me).wait_send()
        kv_copy(peer, me).wait_send()
        q_copy(peer, me).wait_send()
        return carry

    lax.fori_loop(1, n, sent, 0)


def per_device(n, columns, queries, keys, values, dest_replica, dest_slot, doc_lengths, tile_mask):
    q = queries.reshape(NB, BLK, HEADS * WIDTH)
    k = keys.reshape(NB, BLK, WIDTH)
    v = values.reshape(NB, BLK, WIDTH)
    vmem = pl.BlockSpec(memory_space=pltpu.VMEM)
    smem = pl.BlockSpec(memory_space=pltpu.SMEM)
    bf16, f32, i32 = jnp.bfloat16, jnp.float32, jnp.int32
    dma = pltpu.SemaphoreType.DMA
    out = pl.pallas_call(
        functools.partial(kernel, n, columns),
        out_shape=jax.ShapeDtypeStruct((NB, BLK, HEADS * WIDTH), bf16),
        in_specs=[vmem, vmem, vmem, smem, vmem, vmem, vmem, vmem],
        out_specs=vmem,
        scratch_shapes=[
            pltpu.VMEM((n, 2, BLK, WIDTH), bf16),
            pltpu.VMEM((n, 2, BLK, WIDTH), bf16),
            pltpu.VMEM((n, BLK, HEADS * WIDTH), bf16),
            pltpu.VMEM((n, BLK, HEADS * WIDTH), bf16),
            pltpu.VMEM((1, 128), i32),
            pltpu.VMEM((n, 1, 128), i32),
            pltpu.VMEM((3, NB, 2, BLK, WIDTH), bf16),
            pltpu.VMEM((NB, ROWS, 2 * WIDTH), bf16),
            pltpu.VMEM((3, TOK, 2 * WIDTH), bf16),
            pltpu.VMEM((3, TOK, 2 * WIDTH), bf16),
            pltpu.VMEM((NB, 16, 128), bf16),
            pltpu.VMEM((NB, ROWS, 2 * WIDTH), f32),
            pltpu.VMEM((NB, ROWS, 128), f32),
            pltpu.SMEM((NB,), i32),
            dma((n,)), dma((n,)), dma((n,)), dma((n,)), dma((n,)), dma((n,)),
            dma((2, CHUNKS)), dma((2, CHUNKS)),
        ],
        compiler_params=pltpu.CompilerParams(
            collective_id=0, has_side_effects=True, vmem_limit_bytes=48 * 1024 * 1024),
        cost_estimate=pl.CostEstimate(flops=10**10, bytes_accessed=4 * 2**20, transcendentals=10**7),
    )(q, k, v, dest_replica, dest_replica, dest_slot, doc_lengths, tile_mask[0])
    return out.reshape(1, TOK, HEADS * WIDTH)


def solution(mesh):
    n, columns = mesh.shape["dp"], mesh.shape["ctx"]
    return jax.shard_map(
        functools.partial(per_device, n, columns),
        mesh=mesh,
        in_specs=(
            P("dp", "ctx", None),
            P("dp", "ctx", None),
            P("dp", "ctx", None),
            P("dp", "ctx"),
            P("dp", "ctx"),
            P("dp", None),
            P("dp", "ctx", None),
        ),
        out_specs=P("dp", "ctx", None),
        check_vma=False,
    )
```

time: 138 us -> 92.6 us (0.67)
  the two profiles are of different devices: /device:TPU:8 before, /device:TPU:5 now
where the time goes in v1:
time: 92.6 us; the launch traced here: 92.4 us
  Pallas kernels  86.9 us (94%)
  local copies, waits for them, and re-layouts  5.49 us (6%)
    pallas_call x1, Pallas kernels, per_device(): pl.pallas_call(functools.partial(kernel, n, columns), out_shape=jax.Shape...  86.9 us
    unnamed x15, local copies, waits for them, and re-layouts  5.49 us

profile of v1, /device:TPU:5, one launch (start us, length us, event | category | flops | bytes accessed | tf_op | source)
XLA Modules:
  0.0 92.4 jit_solution(16549164244207718634)
XLA Ops:
  0.0 0.0 copy-start.4
  0.0 0.0 copy-start.5
  0.0 0.0 copy-start.6
  0.0 0.6 copy-done.4
  0.7 0.0 copy-done.5
  0.7 0.0 copy-done.6
  0.7 0.0 copy-start
  0.7 1.2 %copy-done = bf16[1,1024,512]{2,1,0:T(8,128)(2,1)S(1)} copy-done((bf16[1,1024,512]{2,1,0:T(8,128)(2,1)S(1)}, bf16[1,1024,512]{2,1,0:T(8,128)(2,1)}, u32[]{:S(2)}) %copy-start) | copy-done | bytes 1048600
  1.9 0.0 copy-start.1
  1.9 0.9 %copy-done.1 = bf16[1,1024,128]{2,1,0:T(8,128)(2,1)S(1)} copy-done((bf16[1,1024,128]{2,1,0:T(8,128)(2,1)S(1)}, bf16[1,1024,128]{2,1,0:T(8,128)(2,1)}, u32[]{:S(2)}) %copy-start.1) | copy-done | bytes 262168
  2.9 0.0 copy-start.2
  2.9 0.9 %copy-done.2 = bf16[1,1024,128]{2,1,0:T(8,128)(2,1)S(1)} copy-done((bf16[1,1024,128]{2,1,0:T(8,128)(2,1)S(1)}, bf16[1,1024,128]{2,1,0:T(8,128)(2,1)}, u32[]{:S(2)}) %copy-start.2) | copy-done | bytes 262168
  3.8 0.0 copy-start.3
  3.8 0.7 copy-done.3
  4.5 86.9 %shard_map.73 = bf16[16,64,512]{2,1,0:T(8,128)(2,1)S(1)} custom-call(bf16[16,64,512]{2,1,0:T(8,128)(2,1)S(1)} %bitcast.6, bf16[16,64,128]{2,1,0:T(8,128)(2,1)S(1)} %bitcast.7, bf16[16,64,128]{2,1,0:T(8,128)(2,1)S(1)} %bitcast.8, s32[1,16]{1,0:T(1,128)S(1)} %copy-done.4, s32[1,16]{1,0:T(1,128)S(1)} %copy-done.4, s32[1,16]{1,0:T(1,128)S(1)} %copy-done.5, ...), custom_call_target="tpu_custom_call" | custom-call | flops 10000000000 | bytes 4194304 | tf_op jit(solution)/shard_map/pallas_call | solution.py:252
  91.4 1.0 %copy.9 = bf16[1,1024,512]{2,1,0:T(8,128)(2,1)} copy(bf16[1,1024,512]{2,1,0:T(8,128)(2,1)S(1)} %bitcast.5) | data formatting | bytes 2097152
Async XLA Ops:
  0.0 0.7 copy-start.4
  0.0 0.7 copy-start.5
  0.0 0.7 copy-start.6
  0.7 1.2 %copy-start = (bf16[1,1024,512]{2,1,0:T(8,128)(2,1)S(1)}, bf16[1,1024,512]{2,1,0:T(8,128)(2,1)}, u32[]{:S(2)}) copy-start(bf16[1,1024,512]{2,1,0:T(8,128)(2,1)} %param.7) | copy-start | bytes 3145732
  1.9 0.9 %copy-start.1 = (bf16[1,1024,128]{2,1,0:T(8,128)(2,1)S(1)}, bf16[1,1024,128]{2,1,0:T(8,128)(2,1)}, u32[]{:S(2)}) copy-start(bf16[1,1024,128]{2,1,0:T(8,128)(2,1)} %param.8) | copy-start | bytes 786436
  2.9 0.9 %copy-start.2 = (bf16[1,1024,128]{2,1,0:T(8,128)(2,1)S(1)}, bf16[1,1024,128]{2,1,0:T(8,128)(2,1)}, u32[]{:S(2)}) copy-start(bf16[1,1024,128]{2,1,0:T(8,128)(2,1)} %param.9) | copy-start | bytes 786436
  3.8 0.7 copy-start.3

commit v2 on v1

v2 whole, which is shorter than its diff:
```python
import functools

import jax
import jax.numpy as jnp
from jax import lax
from jax.experimental import pallas as pl
from jax.experimental.pallas import tpu as pltpu
from jax.sharding import PartitionSpec as P

MESH = pl.DeviceIdType.MESH
HEADS = 4
WIDTH = 128
BLK = 64
NB = 16
TOK = NB * BLK
ROWS = HEADS * BLK
KEYS = 256
SCALE = WIDTH ** (-0.5) * 1.4426950408889634
LOW = -32768.0
CHUNKS = 4
PER = NB // CHUNKS
PAIR = 2
GROUP = PAIR * ROWS
ORDER = (3, 2, 1, 0)
DETOUR = (2, 0)


def tile_bias(col, docs_ref, mask_ref):
    count = docs_ref.shape[1]
    blocks = mask_ref.shape[1]
    lengths = docs_ref[...].astype(jnp.float32)
    upto = lax.broadcasted_iota(jnp.int32, (count, count), 1) <= lax.broadcasted_iota(jnp.int32, (count, count), 0)
    ends = jnp.sum(jnp.where(upto, jnp.broadcast_to(lengths, (count, count)), 0.0), axis=1, keepdims=True)
    block = lax.broadcasted_iota(jnp.int32, (count, blocks), 1).astype(jnp.float32)
    key_doc = jnp.sum(jnp.where(ends <= block, 1.0, 0.0), axis=0, keepdims=True)
    key_doc = jnp.broadcast_to(key_doc, (NB, blocks))
    key_block = lax.broadcasted_iota(jnp.int32, (NB, blocks), 1)
    query_block = lax.broadcasted_iota(jnp.int32, (NB, blocks), 0) + col * NB
    own = key_block == query_block
    query_doc = jnp.sum(jnp.where(own, key_doc, 0.0), axis=1, keepdims=True)
    ok = (key_doc == query_doc) & (key_block <= query_block) & ((mask_ref[...] == 1) | own)
    ok = jnp.where(ok, 1.0, 0.0).astype(jnp.bfloat16)
    window = lax.broadcasted_iota(jnp.int32, (blocks, 128), 1) + (col - 2) * NB
    pick = jnp.where(lax.broadcasted_iota(jnp.int32, (blocks, 128), 0) == window, 1.0, 0.0).astype(jnp.bfloat16)
    ok = jnp.dot(ok, pick, preferred_element_type=jnp.float32)
    return ((1.0 - ok) * LOW).astype(jnp.bfloat16)


def kernel(
    n, columns, q_hbm, k_hbm, v_hbm, rep_hbm, slot_hbm, docs_hbm, mask_hbm, out_ref,
    q_ref, k_ref, v_ref, rep_ref, rep_vec, slot_vec, docs_ref, mask_ref, load_sem,
    kv_send, kv_recv, q_send, q_recv, code_send, code_recv, halo, relay, q_aug, k_aug, v_aug, bias, acc, top, acc_tail, top_tail, src, at, slot_of,
    score_a, high_a, score_b, high_b,
    kv_sent, kv_got, q_sent, q_got, code_sent, code_got, halo_sent, halo_got,
    detour_sent, detour_got, relay_sent,
):
    me = lax.axis_index("dp")
    col = lax.axis_index("ctx")
    last = columns - 1
    bend = columns // 2 - 1
    right = lax.rem(col + 1, columns)
    left = lax.rem(col + columns - 1, columns)

    loads = [
        pltpu.make_async_copy(a, b, load_sem.at[i])
        for i, (a, b) in enumerate((
            (rep_hbm, rep_ref), (rep_hbm, rep_vec), (slot_hbm, slot_vec), (k_hbm, k_ref), (v_hbm, v_ref),
            (q_hbm, q_ref), (docs_hbm, docs_ref), (mask_hbm, mask_ref)))
    ]
    for load in loads:
        load.start()

    barrier = pltpu.get_barrier_semaphore()

    def greet(d, carry):
        pl.semaphore_signal(barrier, inc=1, device_id={"dp": lax.rem(me + d, n)}, device_id_type=MESH)
        return carry

    lax.fori_loop(1, n, greet, 0)

    @pl.when(col > 0)
    def _():
        pl.semaphore_signal(barrier, inc=1, device_id={"ctx": left}, device_id_type=MESH)

    @pl.when(col == last)
    def _():
        pl.semaphore_signal(barrier, inc=1, device_id={"ctx": bend}, device_id_type=MESH)

    @pl.when(col == bend + 1)
    def _():
        pl.semaphore_signal(barrier, inc=1, device_id={"ctx": last}, device_id_type=MESH)

    for load in loads[:5]:
        load.wait()
    code_send[...] = jnp.full((1, 128), -1, jnp.int32)
    code_send[:, :NB] = rep_vec[...] * NB + slot_vec[...] - col * NB

    def block_for(peer):
        where = jnp.int32(0)
        for j in range(NB):
            where = jnp.where(rep_ref[0, j] == peer, j, where)
        return where

    def pack_kv(peer, carry):
        j = block_for(peer)
        kv_send[peer, 0] = k_ref[j]
        kv_send[peer, 1] = v_ref[j]
        return carry

    lax.fori_loop(0, n, pack_kv, 0)

    def kv_copy(peer, slot):
        return pltpu.make_async_remote_copy(
            src_ref=kv_send.at[peer], dst_ref=kv_recv.at[slot], send_sem=kv_sent.at[peer],
            recv_sem=kv_got.at[slot], device_id={"dp": peer}, device_id_type=MESH)

    def q_copy(peer, slot):
        return pltpu.make_async_remote_copy(
            src_ref=q_send.at[peer], dst_ref=q_recv.at[slot], send_sem=q_sent.at[peer],
            recv_sem=q_got.at[slot], device_id={"dp": peer}, device_id_type=MESH)

    def code_copy(peer, slot):
        return pltpu.make_async_remote_copy(
            src_ref=code_send, dst_ref=code_recv.at[slot], send_sem=code_sent.at[peer],
            recv_sem=code_got.at[slot], device_id={"dp": peer}, device_id_type=MESH)

    pl.semaphore_wait(barrier, n + jnp.where(col == bend, 1, 0))

    def send_kv(d, carry):
        peer = lax.rem(me + d, n)
        code_copy(peer, me).start()
        kv_copy(peer, me).start()
        return carry

    lax.fori_loop(1, n, send_kv, 0)
    loads[5].wait()

    def send_q(d, carry):
        peer = lax.rem(me + d, n)
        q_send[peer] = q_ref[block_for(peer)]
        q_copy(peer, me).start()
        return carry

    lax.fori_loop(1, n, send_q, 0)
    mine = block_for(me)
    q_recv[me] = q_ref[mine]
    kv_recv[me, 0] = k_ref[mine]
    kv_recv[me, 1] = v_ref[mine]
    code_recv[me] = code_send[...]

    loads[6].wait()
    loads[7].wait()
    rows = tile_bias(col, docs_ref, mask_ref).astype(jnp.float32)
    for i in range(NB):
        bias[i] = jnp.broadcast_to(rows[i:i + 1], (16, 128)).astype(jnp.bfloat16)
    key_at = lax.broadcasted_iota(jnp.int32, (TOK, 128), 0) // BLK
    lane = lax.broadcasted_iota(jnp.int32, (TOK, 128), 1)
    for p in range(3):
        k_aug[p, :, WIDTH:] = jnp.where(lane == key_at + (2 - p) * NB, 1.0, 0.0).astype(jnp.bfloat16)
        v_aug[p, :, WIDTH:] = jnp.ones((TOK, 128), jnp.bfloat16)
    nothing = jnp.zeros((2, BLK, WIDTH), jnp.bfloat16)
    halo[2, 0] = nothing
    for hop in (1, 2):
        @pl.when(col < hop)
        def _():
            for i in range(NB):
                halo[hop, i] = nothing

    def got_code(d, carry):
        peer = lax.rem(me + n - d, n)
        code_copy(peer, peer).wait_recv()
        return carry

    lax.fori_loop(1, n, got_code, 0)
    codes = code_recv[...].reshape(n, 128)
    sender = lax.broadcasted_iota(jnp.int32, (n, 128), 0)
    for i in range(NB):
        source = jnp.max(jnp.where(codes == me * NB + i, sender, 0))
        src[i] = source
        at[i] = lax.rem(me - source + n, n)
    for d in range(n):
        row = code_recv[lax.rem(me - d + n, n)]
        slot_of[d] = jnp.max(jnp.where((row >= me * NB) & (row < (me + 1) * NB), row - me * NB, 0))

    def got_kv(d, carry):
        peer = lax.rem(me + n - d, n)
        kv_copy(peer, peer).wait_recv()
        return carry

    lax.fori_loop(1, n, got_kv, 0)

    def part_of(hop, chunk):
        return pl.ds(1, PER - 1) if hop == 1 and chunk == 0 else pl.ds(chunk * PER, PER)

    def halo_copy(hop, chunk):
        part = part_of(hop, chunk)
        return pltpu.make_async_remote_copy(
            src_ref=halo.at[hop, part], dst_ref=halo.at[hop + 1, part], send_sem=halo_sent.at[hop, chunk],
            recv_sem=halo_got.at[hop, chunk], device_id={"ctx": right}, device_id_type=MESH)

    def detour_copy(hop, chunk):
        part = part_of(hop, chunk)
        return pltpu.make_async_remote_copy(
            src_ref=halo.at[hop, part], dst_ref=relay.at[hop, part], send_sem=detour_sent.at[hop, chunk],
            recv_sem=detour_got.at[hop, chunk], device_id={"ctx": last}, device_id_type=MESH)

    def relay_copy(hop, chunk):
        part = part_of(hop, chunk)
        return pltpu.make_async_remote_copy(
            src_ref=relay.at[hop, part], dst_ref=halo.at[hop + 1, part], send_sem=relay_sent.at[hop, chunk],
            recv_sem=halo_got.at[hop, chunk], device_id={"ctx": bend + 1}, device_id_type=MESH)

    def send_halo(hop, chunk):
        first = col >= hop
        if chunk in DETOUR:
            @pl.when(first & (col < last) & (col != bend))
            def _():
                halo_copy(hop, chunk).start()

            @pl.when(col == bend)
            def _():
                detour_copy(hop, chunk).start()
        else:
            @pl.when(first & (col < last))
            def _():
                halo_copy(hop, chunk).start()

    def pass_on(hop, chunk):
        @pl.when(col == last)
        def _():
            detour_copy(hop, chunk).wait_recv()
            relay_copy(hop, chunk).start()

    def got_halo(hop, chunk):
        @pl.when(col > hop)
        def _():
            halo_copy(hop, chunk).wait_recv()

    def forward(chunk):
        got_halo(0, chunk)
        send_halo(1, chunk)

    def place_kv(i, carry):
        s = src[i]
        rows = pl.ds(pl.multiple_of(i * BLK, BLK), BLK)
        key, value = kv_recv[s, 0], kv_recv[s, 1]
        halo[0, i, 0] = key
        halo[0, i, 1] = value
        k_aug[0, rows, :WIDTH] = key
        v_aug[0, rows, :WIDTH] = value
        return carry

    for chunk in ORDER:
        lax.fori_loop(chunk * PER, (chunk + 1) * PER, place_kv, 0)
        send_halo(0, chunk)

    def got_q(d):
        peer = lax.rem(me + n - d, n)
        q_copy(peer, peer).wait_recv()

    def wide(value, width):
        return jnp.concatenate([value] * (width // 128), axis=1)

    def score(p, i, lo, hi, buffer, high):
        if p == 0:
            parts = []
            for b in range(PAIR):
                block = q_recv[lax.rem(me - (i + b) + n, n)]
                rows = bias[slot_of[i + b]]
                heads = jnp.concatenate([block[:, h * WIDTH:(h + 1) * WIDTH] for h in range(HEADS)], axis=0)
                part = jnp.concatenate([heads, jnp.concatenate([rows] * (ROWS // 16), axis=0)], axis=1)
                q_aug[i + b] = part
                parts.append(part)
            query = jnp.concatenate(parts, axis=0)
        elif p == 1:
            query = q_aug[pl.ds(i, PAIR)].reshape(GROUP, 2 * WIDTH)
        else:
            query = jnp.concatenate([q_aug[at[i + b]] for b in range(PAIR)], axis=0)
        width = hi - lo
        value = lax.dot_general(
            query, k_aug[min(p, 2), lo:hi, :], (((1,), (1,)), ((), ())), preferred_element_type=jnp.float32)
        if p == 0:
            row = lax.broadcasted_iota(jnp.int32, (GROUP, 128), 0)
            upto = lax.rem(row, BLK) + jnp.where(row < ROWS, slot_of[i], slot_of[i + 1]) * BLK
            key = lax.broadcasted_iota(jnp.int32, (GROUP, TOK), 1)
            value = jnp.where(key <= wide(upto, TOK), value, LOW)
        buffer[:, :width] = value
        most = value[:, :128]
        for c in range(128, width, 128):
            most = jnp.maximum(most, value[:, c:c + 128])
        high[...] = jnp.broadcast_to(jnp.max(most, axis=1, keepdims=True), (GROUP, 128))

    def soft(p, i, lo, hi, buffer, high):
        width = hi - lo
        most = high[...]
        total = None
        if p == 1:
            before = top[pl.ds(i, PAIR)].reshape(GROUP, 128)
            total = acc[pl.ds(i, PAIR)].reshape(GROUP, 2 * WIDTH)
        elif p in (2, 3):
            before = jnp.concatenate([top[at[i + b]] for b in range(PAIR)], axis=0)
            total = jnp.concatenate([acc[at[i + b]] for b in range(PAIR)], axis=0)
        elif p == 4:
            before = top_tail[pl.ds(i, PAIR)].reshape(GROUP, 128)
            total = acc_tail[pl.ds(i, PAIR)].reshape(GROUP, 2 * WIDTH)
        if total is not None:
            most = jnp.maximum(most, before)
        weight = jnp.exp2((buffer[:, :width] - wide(most, width)) * SCALE)
        part = jnp.dot(
            weight.astype(jnp.bfloat16), v_aug[min(p, 2), lo:hi, :], preferred_element_type=jnp.float32)
        if total is not None:
            factor = jnp.exp2((before - most) * SCALE)
            part = part + total * wide(factor, 2 * WIDTH)
        if p < 2:
            acc[pl.ds(i, PAIR)] = part.reshape(PAIR, ROWS, 2 * WIDTH)
            top[pl.ds(i, PAIR)] = most.reshape(PAIR, ROWS, 128)
        elif p == 3:
            acc_tail[pl.ds(i, PAIR)] = part.reshape(PAIR, ROWS, 2 * WIDTH)
            top_tail[pl.ds(i, PAIR)] = most.reshape(PAIR, ROWS, 128)
        else:
            result = (part[:, :WIDTH] / part[:, WIDTH:]).astype(jnp.bfloat16)
            for b in range(PAIR):
                for h in range(HEADS):
                    first = b * ROWS + h * BLK
                    out_ref[i + b, :, h * WIDTH:(h + 1) * WIDTH] = result[first:first + BLK]

    def take_halo(hop, chunk):
        for i in range(chunk * PER, (chunk + 1) * PER):
            k_aug[hop, i * BLK:(i + 1) * BLK, :WIDTH] = halo[hop, i, 0]
            v_aug[hop, i * BLK:(i + 1) * BLK, :WIDTH] = halo[hop, i, 1]

    def second(chunk):
        got_halo(1, chunk)
        take_halo(2, chunk)

    def arrive():
        for chunk in ORDER:
            take_halo(1, chunk)

    steps = [(0, i, 0, TOK) for i in range(0, NB, PAIR)]
    count = len(steps)
    steps += [(1, i, 0, TOK) for i in range(0, NB, PAIR)]
    steps += [(2, i, min((i + 1) // PER, 3) * KEYS, TOK) for i in range(NB - PAIR, PER - 1, -PAIR)]
    steps += [(3, i, KEYS, TOK) for i in range(PER - PAIR, -1, -PAIR)]
    final = len(steps)
    steps += [(4, i, 0, KEYS) for i in range(PER - PAIR, -1, -PAIR)]
    before = {k: [] for k in range(len(steps))}
    for k in range(count):
        for b in range(PAIR):
            if k * PAIR + b:
                before[k].append(functools.partial(got_q, k * PAIR + b))
    before[2] += [lambda: pass_on(0, 2), lambda: forward(3)]
    before[4] += [lambda: forward(2)]
    before[5] += [lambda: pass_on(0, 0)]
    before[6] += [lambda: forward(1)]
    before[7] += [lambda: pass_on(1, 2)]
    before[count] += [lambda: forward(0), arrive]
    before[count + 1] += [lambda: pass_on(1, 0)]
    before[2 * count] += [lambda: second(3)]
    before[2 * count + 2] += [lambda: second(2)]
    before[2 * count + 4] += [lambda: second(1)]
    before[final] += [lambda: second(0)]
    buffers = ((score_a, high_a), (score_b, high_b))
    for act in before[0]:
        act()
    score(*steps[0], *buffers[0])
    k = 0
    while k < len(steps):
        for act in before.get(k + 1, ()):
            act()
        if k == count:
            def two(j, carry):
                for u in range(2):
                    i = (2 * j + u) * PAIR
                    score(1, i + PAIR, 0, TOK, *buffers[(u + 1) % 2])
                    soft(1, i, 0, TOK, *buffers[u])
                return carry

            lax.fori_loop(0, count // 2 - 1, two, 0)
            k = 2 * count - 2
        if k + 1 < len(steps):
            score(*steps[k + 1], *buffers[(k + 1) % 2])
        soft(*steps[k], *buffers[k % 2])
        k += 1

    for hop in range(2):
        for chunk in range(CHUNKS):
            first = col >= hop
            if chunk in DETOUR:
                @pl.when(first & (col < last) & (col != bend))
                def _():
                    halo_copy(hop, chunk).wait_send()

                @pl.when(col == bend)
                def _():
                    detour_copy(hop, chunk).wait_send()

                @pl.when(col == last)
                def _():
                    relay_copy(hop, chunk).wait_send()
            else:
                @pl.when(first & (col < last))
                def _():
                    halo_copy(hop, chunk).wait_send()

    def sent(d, carry):
        peer = lax.rem(me + d, n)
        code_copy(peer, me).wait_send()
        kv_copy(peer, me).wait_send()
        q_copy(peer, me).wait_send()
        return carry

    lax.fori_loop(1, n, sent, 0)


def per_device(n, columns, queries, keys, values, dest_replica, dest_slot, doc_lengths, tile_mask):
    q = queries.reshape(NB, BLK, HEADS * WIDTH)
    k = keys.reshape(NB, BLK, WIDTH)
    v = values.reshape(NB, BLK, WIDTH)
    vmem, smem = pltpu.VMEM, pltpu.SMEM
    bf16, f32, i32 = jnp.bfloat16, jnp.float32, jnp.int32
    dma = pltpu.SemaphoreType.DMA
    out = pl.pallas_call(
        functools.partial(kernel, n, columns),
        out_shape=jax.ShapeDtypeStruct((NB, BLK, HEADS * WIDTH), bf16),
        in_specs=[pl.BlockSpec(memory_space=pltpu.HBM)] * 7,
        out_specs=pl.BlockSpec(memory_space=vmem),
        scratch_shapes=[
            vmem(q.shape, bf16), vmem(k.shape, bf16), vmem(v.shape, bf16),
            smem(dest_replica.shape, i32), vmem(dest_replica.shape, i32), vmem(dest_slot.shape, i32),
            vmem(doc_lengths.shape, i32), vmem(tile_mask.shape[1:], i32), dma((8,)),
            vmem((n, 2, BLK, WIDTH), bf16),
            vmem((n, 2, BLK, WIDTH), bf16),
            vmem((n, BLK, HEADS * WIDTH), bf16),
            vmem((n, BLK, HEADS * WIDTH), bf16),
            vmem((1, 128), i32),
            vmem((n, 1, 128), i32),
            vmem((3, NB, 2, BLK, WIDTH), bf16),
            vmem((2, NB, 2, BLK, WIDTH), bf16),
            vmem((NB, ROWS, 2 * WIDTH), bf16),
            vmem((3, TOK, 2 * WIDTH), bf16),
            vmem((3, TOK, 2 * WIDTH), bf16),
            vmem((NB, 16, 128), bf16),
            vmem((NB, ROWS, 2 * WIDTH), f32),
            vmem((NB, ROWS, 128), f32),
            vmem((PER, ROWS, 2 * WIDTH), f32),
            vmem((PER, ROWS, 128), f32),
            smem((NB,), i32), smem((NB,), i32), smem((NB,), i32),
            vmem((GROUP, TOK), f32), vmem((GROUP, 128), f32), vmem((GROUP, TOK), f32), vmem((GROUP, 128), f32),
            dma((n,)), dma((n,)), dma((n,)), dma((n,)), dma((n,)), dma((n,)),
            dma((2, CHUNKS)), dma((2, CHUNKS)), dma((2, CHUNKS)), dma((2, CHUNKS)), dma((2, CHUNKS)),
        ],
        compiler_params=pltpu.CompilerParams(
            collective_id=0, has_side_effects=True, vmem_limit_bytes=56 * 1024 * 1024),
        cost_estimate=pl.CostEstimate(flops=10**10, bytes_accessed=4 * 2**20, transcendentals=10**7),
    )(q, k, v, dest_replica, dest_slot, doc_lengths, tile_mask[0])
    return out.reshape(1, TOK, HEADS * WIDTH)


def solution(mesh):
    n, columns = mesh.shape["dp"], mesh.shape["ctx"]
    return jax.shard_map(
        functools.partial(per_device, n, columns),
        mesh=mesh,
        in_specs=(
            P("dp", "ctx", None),
            P("dp", "ctx", None),
            P("dp", "ctx", None),
            P("dp", "ctx"),
            P("dp", "ctx"),
            P("dp", None),
            P("dp", "ctx", None),
        ),
        out_specs=P("dp", "ctx", None),
        check_vma=False,
    )
```

time: 92.6 us -> 56.5 us (0.61)
  the two profiles are of different devices: /device:TPU:5 before, /device:TPU:8 now
where the time goes in v2:
time: 56.5 us; the launch traced here: 56.2 us
  Pallas kernels  53.9 us (95%)
  local copies, waits for them, and re-layouts  2.26 us (4%)
    pallas_call x1, Pallas kernels, per_device(): pl.pallas_call(functools.partial(kernel, n, columns), out_shape=jax.Shape...  53.9 us
    unnamed x1, local copies, waits for them, and re-layouts  2.26 us

profile of v2, /device:TPU:8, one launch (start us, length us, event | category | flops | bytes accessed | tf_op | source)
XLA Modules:
  0.0 56.2 jit_solution(9435138202845799535)
XLA Ops:
  0.0 53.9 %shard_map.73 = bf16[16,64,512]{2,1,0:T(8,128)(2,1)} custom-call(bf16[16,64,512]{2,1,0:T(8,128)(2,1)} %bitcast.6, bf16[16,64,128]{2,1,0:T(8,128)(2,1)} %bitcast.7, bf16[16,64,128]{2,1,0:T(8,128)(2,1)} %bitcast.8, s32[1,16]{1,0:T(1,128)} %rep_hbm.1, s32[1,16]{1,0:T(1,128)} %slot_hbm.1, s32[1,64]{1,0:T(1,128)} %docs_hbm.1, s32[16,256]{1,0:T(8,128)} %bitcast.9), custom_call_target="tpu_custom_call" | custom-call | flops 10000000000 | bytes 4194304 | tf_op jit(solution)/shard_map/pallas_call | solution.py:423
  54.0 2.3 %copy.9 = bf16[1,1024,512]{2,1,0:T(8,128)(2,1)} copy(bf16[1,1024,512]{2,1,0:T(8,128)(2,1)} %bitcast.5) | data formatting | bytes 2097152

commit v3 on v2

--- a/solution.py
+++ b/solution.py
@@ -22,7 +22,13 @@
 PAIR = 2
 GROUP = PAIR * ROWS
 ORDER = (3, 2, 1, 0)
-DETOUR = (2, 0)
+BY_LAST = ((), (2, 1, 0))
+STEPS = (
+    (0, 0, 1), (1, 0, 0), (3, 0, 1), (0, 1, 0), (2, 1, 1),
+    (1, 1, 0), (3, 1, 1), (2, 0, 0), (1, 0, 1), (3, 0, 0),
+    (2, 1, 0), (1, 1, 1), (3, 1, 0), (2, 0, 1), (0, 1, 1),
+)
+BATCHES = ((1, 6), (6, 11), (11, 16))
 
 
 def tile_bias(col, docs_ref, mask_ref):
@@ -61,6 +67,18 @@
     right = lax.rem(col + 1, columns)
     left = lax.rem(col + columns - 1, columns)
 
+    spots = (me // 4, lax.rem(me // 2, 2), lax.rem(me, 2))
+
+    def partner(d, sign):
+        if d == 0:
+            return me
+        dx, dy, dc = STEPS[d - 1]
+        x = lax.rem(spots[0] + (4 + sign * dx), 4)
+        return (x * 2 + lax.rem(spots[1] + dy, 2)) * 2 + lax.rem(spots[2] + dc, 2)
+
+    targets = [partner(d, 1) for d in range(n)]
+    sources = [partner(d, -1) for d in range(n)]
+
     loads = [
         pltpu.make_async_copy(a, b, load_sem.at[i])
         for i, (a, b) in enumerate((
@@ -82,13 +100,10 @@
     def _():
         pl.semaphore_signal(barrier, inc=1, device_id={"ctx": left}, device_id_type=MESH)
 
-    @pl.when(col == last)
-    def _():
-        pl.semaphore_signal(barrier, inc=1, device_id={"ctx": bend}, device_id_type=MESH)
-
-    @pl.when(col == bend + 1)
-    def _():
-        pl.semaphore_signal(barrier, inc=1, device_id={"ctx": last}, device_id_type=MESH)
+    for here, there in ((last, bend), (bend + 1, last)):
+        @pl.when(col == here)
+        def _():
+            pl.semaphore_signal(barrier, inc=1, device_id={"ctx": there}, device_id_type=MESH)
 
     for load in loads[:5]:
         load.wait()
@@ -101,13 +116,10 @@
             where = jnp.where(rep_ref[0, j] == peer, j, where)
         return where
 
-    def pack_kv(peer, carry):
-        j = block_for(peer)
-        kv_send[peer, 0] = k_ref[j]
-        kv_send[peer, 1] = v_ref[j]
-        return carry
-
-    lax.fori_loop(0, n, pack_kv, 0)
+    held = [block_for(peer) for peer in targets]
+    for d in range(1, n):
+        kv_send[targets[d], 0] = k_ref[held[d]]
+        kv_send[targets[d], 1] = v_ref[held[d]]
 
     def kv_copy(peer, slot):
         return pltpu.make_async_remote_copy(
@@ -126,23 +138,25 @@
 
     pl.semaphore_wait(barrier, n + jnp.where(col == bend, 1, 0))
 
-    def send_kv(d, carry):
-        peer = lax.rem(me + d, n)
-        code_copy(peer, me).start()
-        kv_copy(peer, me).start()
-        return carry
-
-    lax.fori_loop(1, n, send_kv, 0)
+    for d in range(1, n):
+        code_copy(targets[d], me).start()
+        kv_copy(targets[d], me).start()
     loads[5].wait()
 
-    def send_q(d, carry):
-        peer = lax.rem(me + d, n)
-        q_send[peer] = q_ref[block_for(peer)]
-        q_copy(peer, me).start()
-        return carry
-
-    lax.fori_loop(1, n, send_q, 0)
-    mine = block_for(me)
+    def send_q(batch):
+        for d in range(*BATCHES[batch]):
+            q_send[targets[d]] = q_ref[held[d]]
+            q_copy(targets[d], me).start()
+
+    send_q(0)
+    early = (col == 0) | (col == bend) | (col == bend + 1)
+
+    @pl.when(early)
+    def _():
+        send_q(1)
+        send_q(2)
+
+    mine = held[0]
     q_recv[me] = q_ref[mine]
     kv_recv[me, 0] = k_ref[mine]
     kv_recv[me, 1] = v_ref[mine]
@@ -166,28 +180,22 @@
             for i in range(NB):
                 halo[hop, i] = nothing
 
-    def got_code(d, carry):
-        peer = lax.rem(me + n - d, n)
-        code_copy(peer, peer).wait_recv()
-        return carry
-
-    lax.fori_loop(1, n, got_code, 0)
+    for d in range(1, n):
+        code_copy(sources[d], sources[d]).wait_recv()
     codes = code_recv[...].reshape(n, 128)
     sender = lax.broadcasted_iota(jnp.int32, (n, 128), 0)
     for i in range(NB):
         source = jnp.max(jnp.where(codes == me * NB + i, sender, 0))
         src[i] = source
-        at[i] = lax.rem(me - source + n, n)
+        order = jnp.int32(0)
+        for d in range(1, n):
+            order = jnp.where(source == sources[d], d, order)
+        at[i] = order
     for d in range(n):
-        row = code_recv[lax.rem(me - d + n, n)]
+        row = code_recv[sources[d]]
         slot_of[d] = jnp.max(jnp.where((row >= me * NB) & (row < (me + 1) * NB), row - me * NB, 0))
-
-    def got_kv(d, carry):
-        peer = lax.rem(me + n - d, n)
-        kv_copy(peer, peer).wait_recv()
-        return carry
-
-    lax.fori_loop(1, n, got_kv, 0)
+    for d in range(1, n):
+        kv_copy(sources[d], sources[d]).wait_recv()
 
     def part_of(hop, chunk):
         return pl.ds(1, PER - 1) if hop == 1 and chunk == 0 else pl.ds(chunk * PER, PER)
@@ -198,11 +206,14 @@
             src_ref=halo.at[hop, part], dst_ref=halo.at[hop + 1, part], send_sem=halo_sent.at[hop, chunk],
             recv_sem=halo_got.at[hop, chunk], device_id={"ctx": right}, device_id_type=MESH)
 
+    def detour_of(hop, chunk):
+        return last if chunk in BY_LAST[hop] else None
+
     def detour_copy(hop, chunk):
         part = part_of(hop, chunk)
         return pltpu.make_async_remote_copy(
             src_ref=halo.at[hop, part], dst_ref=relay.at[hop, part], send_sem=detour_sent.at[hop, chunk],
-            recv_sem=detour_got.at[hop, chunk], device_id={"ctx": last}, device_id_type=MESH)
+            recv_sem=detour_got.at[hop, chunk], device_id={"ctx": detour_of(hop, chunk)}, device_id_type=MESH)
 
     def relay_copy(hop, chunk):
         part = part_of(hop, chunk)
@@ -210,35 +221,44 @@
             src_ref=relay.at[hop, part], dst_ref=halo.at[hop + 1, part], send_sem=relay_sent.at[hop, chunk],
             recv_sem=halo_got.at[hop, chunk], device_id={"ctx": bend + 1}, device_id_type=MESH)
 
+    def sends(hop, chunk):
+        to_right = (col >= hop) & (col < last)
+        if detour_of(hop, chunk) is not None:
+            to_right = to_right & (col != bend)
+        return to_right
+
     def send_halo(hop, chunk):
-        first = col >= hop
-        if chunk in DETOUR:
-            @pl.when(first & (col < last) & (col != bend))
-            def _():
-                halo_copy(hop, chunk).start()
-
+        @pl.when(sends(hop, chunk))
+        def _():
+            halo_copy(hop, chunk).start()
+
+        if detour_of(hop, chunk) is not None:
             @pl.when(col == bend)
             def _():
                 detour_copy(hop, chunk).start()
-        else:
-            @pl.when(first & (col < last))
-            def _():
-                halo_copy(hop, chunk).start()
 
     def pass_on(hop, chunk):
-        @pl.when(col == last)
+        @pl.when(col == detour_of(hop, chunk))
         def _():
             detour_copy(hop, chunk).wait_recv()
             relay_copy(hop, chunk).start()
 
-    def got_halo(hop, chunk):
-        @pl.when(col > hop)
-        def _():
-            halo_copy(hop, chunk).wait_recv()
-
     def forward(chunk):
-        got_halo(0, chunk)
-        send_halo(1, chunk)
+        @pl.when(col > 0)
+        def _():
+            halo_copy(0, chunk).wait_recv()
+
+        if detour_of(1, chunk) is None:
+            @pl.when(sends(1, chunk) & (col != bend))
+            def _():
+                halo_copy(1, chunk).start()
+        else:
+            send_halo(1, chunk)
+
+    def cross(chunk):
+        @pl.when(col == bend)
+        def _():
+            halo_copy(1, chunk).start()
 
     def place_kv(i, carry):
         s = src[i]
@@ -255,8 +275,7 @@
         send_halo(0, chunk)
 
     def got_q(d):
-        peer = lax.rem(me + n - d, n)
-        q_copy(peer, peer).wait_recv()
+        q_copy(sources[d], sources[d]).wait_recv()
 
     def wide(value, width):
         return jnp.concatenate([value] * (width // 128), axis=1)
@@ -265,7 +284,7 @@
         if p == 0:
             parts = []
             for b in range(PAIR):
-                block = q_recv[lax.rem(me - (i + b) + n, n)]
+                block = q_recv[sources[i + b]]
                 rows = bias[slot_of[i + b]]
                 heads = jnp.concatenate([block[:, h * WIDTH:(h + 1) * WIDTH] for h in range(HEADS)], axis=0)
                 part = jnp.concatenate([heads, jnp.concatenate([rows] * (ROWS // 16), axis=0)], axis=1)
@@ -289,6 +308,13 @@
         for c in range(128, width, 128):
             most = jnp.maximum(most, value[:, c:c + 128])
         high[...] = jnp.broadcast_to(jnp.max(most, axis=1, keepdims=True), (GROUP, 128))
+
+    def finish(i, part):
+        result = (part[:, :WIDTH] / part[:, WIDTH:]).astype(jnp.bfloat16)
+        for b in range(PAIR):
+            for h in range(HEADS):
+                first = b * ROWS + h * BLK
+                out_ref[i + b, :, h * WIDTH:(h + 1) * WIDTH] = result[first:first + BLK]
 
     def soft(p, i, lo, hi, buffer, high):
         width = hi - lo
@@ -318,11 +344,7 @@
             acc_tail[pl.ds(i, PAIR)] = part.reshape(PAIR, ROWS, 2 * WIDTH)
             top_tail[pl.ds(i, PAIR)] = most.reshape(PAIR, ROWS, 128)
         else:
-            result = (part[:, :WIDTH] / part[:, WIDTH:]).astype(jnp.bfloat16)
-            for b in range(PAIR):
-                for h in range(HEADS):
-                    first = b * ROWS + h * BLK
-                    out_ref[i + b, :, h * WIDTH:(h + 1) * WIDTH] = result[first:first + BLK]
+            finish(i, part)
 
     def take_halo(hop, chunk):
         for i in range(chunk * PER, (chunk + 1) * PER):
@@ -330,7 +352,9 @@
             v_aug[hop, i * BLK:(i + 1) * BLK, :WIDTH] = halo[hop, i, 1]
 
     def second(chunk):
-        got_halo(1, chunk)
+        @pl.when(col > 1)
+        def _():
+            halo_copy(1, chunk).wait_recv()
         take_halo(2, chunk)
 
     def arrive():
@@ -349,13 +373,24 @@
         for b in range(PAIR):
             if k * PAIR + b:
                 before[k].append(functools.partial(got_q, k * PAIR + b))
-    before[2] += [lambda: pass_on(0, 2), lambda: forward(3)]
-    before[4] += [lambda: forward(2)]
-    before[5] += [lambda: pass_on(0, 0)]
-    before[6] += [lambda: forward(1)]
-    before[7] += [lambda: pass_on(1, 2)]
-    before[count] += [lambda: forward(0), arrive]
-    before[count + 1] += [lambda: pass_on(1, 0)]
+    @pl.when(jnp.logical_not(early))
+    def _():
+        send_q(1)
+
+    for d in range(*BATCHES[0]):
+        q_copy(targets[d], me).wait_send()
+
+    @pl.when(jnp.logical_not(early))
+    def _():
+        send_q(2)
+
+    forward(3)
+    before[2] += [lambda: forward(2)]
+    before[5] += [lambda: forward(1)]
+    before[count] += [lambda: forward(0), lambda: cross(3), arrive]
+    before[count + 1] += [lambda: pass_on(1, 2)]
+    before[count + 3] += [lambda: pass_on(1, 1)]
+    before[count + 6] += [lambda: pass_on(1, 0)]
     before[2 * count] += [lambda: second(3)]
     before[2 * count + 2] += [lambda: second(2)]
     before[2 * count + 4] += [lambda: second(1)]
@@ -368,49 +403,47 @@
     while k < len(steps):
         for act in before.get(k + 1, ()):
             act()
-        if k == count:
-            def two(j, carry):
-                for u in range(2):
-                    i = (2 * j + u) * PAIR
-                    score(1, i + PAIR, 0, TOK, *buffers[(u + 1) % 2])
-                    soft(1, i, 0, TOK, *buffers[u])
-                return carry
-
-            lax.fori_loop(0, count // 2 - 1, two, 0)
-            k = 2 * count - 2
-        if k + 1 < len(steps):
-            score(*steps[k + 1], *buffers[(k + 1) % 2])
-        soft(*steps[k], *buffers[k % 2])
+        def advance(k=k):
+            if k + 1 < len(steps):
+                score(*steps[k + 1], *buffers[(k + 1) % 2])
+            soft(*steps[k], *buffers[k % 2])
+
+        if k < count:
+            advance()
+        else:
+            pl.when(col > 0)(advance)
         k += 1
+
+    @pl.when(col == 0)
+    def _():
+        def alone(j, carry):
+            i = j * PAIR
+            finish(i, jnp.concatenate([acc[at[i + b]] for b in range(PAIR)], axis=0))
+            return carry
+
+        lax.fori_loop(0, NB // PAIR, alone, 0)
 
     for hop in range(2):
         for chunk in range(CHUNKS):
-            first = col >= hop
-            if chunk in DETOUR:
-                @pl.when(first & (col < last) & (col != bend))
-                def _():
-                    halo_copy(hop, chunk).wait_send()
-
+            @pl.when(sends(hop, chunk))
+            def _():
+                halo_copy(hop, chunk).wait_send()
+
+            via = detour_of(hop, chunk)
+            if via is not None:
                 @pl.when(col == bend)
                 def _():
                     detour_copy(hop, chunk).wait_send()
 
-                @pl.when(col == last)
+                @pl.when(col == via)
                 def _():
                     relay_copy(hop, chunk).wait_send()
-            else:
-                @pl.when(first & (col < last))
-                def _():
-                    halo_copy(hop, chunk).wait_send()
-
-    def sent(d, carry):
-        peer = lax.rem(me + d, n)
-        code_copy(peer, me).wait_send()
-        kv_copy(peer, me).wait_send()
-        q_copy(peer, me).wait_send()
-        return carry
-
-    lax.fori_loop(1, n, sent, 0)
+
+    for d in range(1, n):
+        code_copy(targets[d], me).wait_send()
+        kv_copy(targets[d], me).wait_send()
+    for d in range(BATCHES[1][0], n):
+        q_copy(targets[d], me).wait_send()
 
 
 def per_device(n, columns, queries, keys, values, dest_replica, dest_slot, doc_lengths, tile_mask):

time: 56.5 us -> 51.8 us (0.917); the launches traced: 56.2 us -> 50.9 us
  Pallas kernels: 53.9 us -> 48.6 us
    pallas_call x1, Pallas kernels: 53.9 us -> 48.6 us  [per_device(): pl.pallas_call(functools.partial(kernel, n, columns), out_shape=jax.Shape...]
where the time goes in v3:
time: 51.8 us; the launch traced here: 50.9 us
  Pallas kernels  48.6 us (94%)
  local copies, waits for them, and re-layouts  2.26 us (4%)
    pallas_call x1, Pallas kernels, per_device(): pl.pallas_call(functools.partial(kernel, n, columns), out_shape=jax.Shape...  48.6 us
    unnamed x1, local copies, waits for them, and re-layouts  2.26 us

profile of v3, /device:TPU:8, one launch (start us, length us, event | category | flops | bytes accessed | tf_op | source)
XLA Modules:
  0.0 50.9 jit_solution(8333982791489354432)
XLA Ops:
  0.0 48.6 %shard_map.73 = bf16[16,64,512]{2,1,0:T(8,128)(2,1)} custom-call(bf16[16,64,512]{2,1,0:T(8,128)(2,1)} %bitcast.6, bf16[16,64,128]{2,1,0:T(8,128)(2,1)} %bitcast.7, bf16[16,64,128]{2,1,0:T(8,128)(2,1)} %bitcast.8, s32[1,16]{1,0:T(1,128)} %rep_hbm.1, s32[1,16]{1,0:T(1,128)} %slot_hbm.1, s32[1,64]{1,0:T(1,128)} %docs_hbm.1, s32[16,256]{1,0:T(8,128)} %bitcast.9), custom_call_target="tpu_custom_call" | custom-call | flops 10000000000 | bytes 4194304 | tf_op jit(solution)/shard_map/pallas_call | solution.py:456
  48.6 2.3 %copy.9 = bf16[1,1024,512]{2,1,0:T(8,128)(2,1)} copy(bf16[1,1024,512]{2,1,0:T(8,128)(2,1)} %bitcast.5) | data formatting | bytes 2097152

commit v4 on v3

--- a/solution.py
+++ b/solution.py
@@ -22,7 +22,7 @@
 PAIR = 2
 GROUP = PAIR * ROWS
 ORDER = (3, 2, 1, 0)
-BY_LAST = ((), (2, 1, 0))
+BY_LAST = ((), (1, 0))
 STEPS = (
     (0, 0, 1), (1, 0, 0), (3, 0, 1), (0, 1, 0), (2, 1, 1),
     (1, 1, 0), (3, 1, 1), (2, 0, 0), (1, 0, 1), (3, 0, 0),
@@ -243,17 +243,20 @@
             detour_copy(hop, chunk).wait_recv()
             relay_copy(hop, chunk).start()
 
-    def forward(chunk):
-        @pl.when(col > 0)
+    def forward(chunk, here=None):
+        @pl.when(col > 0 if here is None else (col > 0) & here)
         def _():
             halo_copy(0, chunk).wait_recv()
 
-        if detour_of(1, chunk) is None:
-            @pl.when(sends(1, chunk) & (col != bend))
+        right_now = sends(1, chunk) & (col != bend)
+        @pl.when(right_now if here is None else right_now & here)
+        def _():
+            halo_copy(1, chunk).start()
+
+        if detour_of(1, chunk) is not None:
+            @pl.when(col == bend if here is None else (col == bend) & here)
             def _():
-                halo_copy(1, chunk).start()
-        else:
-            send_halo(1, chunk)
+                detour_copy(1, chunk).start()
 
     def cross(chunk):
         @pl.when(col == bend)
@@ -272,7 +275,20 @@
 
     for chunk in ORDER:
         lax.fori_loop(chunk * PER, (chunk + 1) * PER, place_kv, 0)
-        send_halo(0, chunk)
+        if chunk in (3, 2):
+            send_halo(0, chunk)
+        else:
+            @pl.when(sends(0, chunk) & (col != bend))
+            def _():
+                halo_copy(0, chunk).start()
+
+    def second_part():
+        @pl.when(col == bend)
+        def _():
+            for chunk in (3, 2):
+                halo_copy(0, chunk).wait_send()
+            for chunk in (1, 0):
+                halo_copy(0, chunk).start()
 
     def got_q(d):
         q_copy(sources[d], sources[d]).wait_recv()
@@ -357,13 +373,15 @@
             halo_copy(1, chunk).wait_recv()
         take_halo(2, chunk)
 
-    def arrive():
-        for chunk in ORDER:
+    def arrive(*chunks):
+        for chunk in chunks:
             take_halo(1, chunk)
 
     steps = [(0, i, 0, TOK) for i in range(0, NB, PAIR)]
     count = len(steps)
-    steps += [(1, i, 0, TOK) for i in range(0, NB, PAIR)]
+    half = TOK // 2
+    steps += [(1, i, half, TOK) for i in range(0, NB, PAIR)] + [(1, i, 0, half) for i in range(0, NB, PAIR)]
+    other = len(steps)
     steps += [(2, i, min((i + 1) // PER, 3) * KEYS, TOK) for i in range(NB - PAIR, PER - 1, -PAIR)]
     steps += [(3, i, KEYS, TOK) for i in range(PER - PAIR, -1, -PAIR)]
     final = len(steps)
@@ -384,16 +402,21 @@
     def _():
         send_q(2)
 
-    forward(3)
-    before[2] += [lambda: forward(2)]
-    before[5] += [lambda: forward(1)]
-    before[count] += [lambda: forward(0), lambda: cross(3), arrive]
-    before[count + 1] += [lambda: pass_on(1, 2)]
-    before[count + 3] += [lambda: pass_on(1, 1)]
-    before[count + 6] += [lambda: pass_on(1, 0)]
-    before[2 * count] += [lambda: second(3)]
-    before[2 * count + 2] += [lambda: second(2)]
-    before[2 * count + 4] += [lambda: second(1)]
+    forward(3, col != bend + 1)
+    far = col == bend + 1
+    near = col != bend + 1
+    before[2] += [lambda: forward(2, near)]
+    before[5] += [lambda: forward(1, near)]
+    before[6] += [lambda: forward(3, far)]
+    before[7] += [lambda: forward(2, far)]
+    before[2] += [second_part]
+    before[count] += [lambda: forward(0, near), lambda: cross(3), lambda: cross(2), lambda: arrive(3, 2)]
+    before[count + 6] += [lambda: pass_on(1, 1)]
+    before[count + 8] += [lambda: forward(1, far), lambda: forward(0, far), lambda: arrive(1, 0)]
+    before[count + 11] += [lambda: pass_on(1, 0)]
+    before[other] += [lambda: second(3)]
+    before[other + 2] += [lambda: second(2)]
+    before[other + 4] += [lambda: second(1)]
     before[final] += [lambda: second(0)]
     buffers = ((score_a, high_a), (score_b, high_b))
     for act in before[0]:
@@ -425,7 +448,9 @@
 
     for hop in range(2):
         for chunk in range(CHUNKS):
-            @pl.when(sends(hop, chunk))
+            taken = hop == 0 and chunk in (3, 2)
+
+            @pl.when(sends(hop, chunk) & (col != bend) if taken else sends(hop, chunk))
             def _():
                 halo_copy(hop, chunk).wait_send()
 

time: 51.8 us -> 50.7 us (0.979); the launches traced: 50.9 us -> 50.5 us
  no operation moved by 1% of the time
where the time goes in v4:
time: 50.7 us; the launch traced here: 50.5 us
  Pallas kernels  48.3 us (95%)
  local copies, waits for them, and re-layouts  2.26 us (4%)
    pallas_call x1, Pallas kernels, per_device(): pl.pallas_call(functools.partial(kernel, n, columns), out_shape=jax.Shape...  48.3 us
    unnamed x1, local copies, waits for them, and re-layouts  2.26 us

profile of v4, /device:TPU:8, one launch (start us, length us, event | category | flops | bytes accessed | tf_op | source)
XLA Modules:
  0.0 50.5 jit_solution(10358728034195469265)
XLA Ops:
  0.0 48.3 %shard_map.73 = bf16[16,64,512]{2,1,0:T(8,128)(2,1)} custom-call(bf16[16,64,512]{2,1,0:T(8,128)(2,1)} %bitcast.6, bf16[16,64,128]{2,1,0:T(8,128)(2,1)} %bitcast.7, bf16[16,64,128]{2,1,0:T(8,128)(2,1)} %bitcast.8, s32[1,16]{1,0:T(1,128)} %rep_hbm.1, s32[1,16]{1,0:T(1,128)} %slot_hbm.1, s32[1,64]{1,0:T(1,128)} %docs_hbm.1, s32[16,256]{1,0:T(8,128)} %bitcast.9), custom_call_target="tpu_custom_call" | custom-call | flops 10000000000 | bytes 4194304 | tf_op jit(solution)/shard_map/pallas_call | solution.py:481
  48.3 2.3 %copy.9 = bf16[1,1024,512]{2,1,0:T(8,128)(2,1)} copy(bf16[1,1024,512]{2,1,0:T(8,128)(2,1)} %bitcast.5) | data formatting | bytes 2097152
